TPU v7x, 512 devices: a whole 4x4x16 slice. The times are simulated.
512 devices in a mesh: section: 4 (over y), seq: 128 (over x, z, core).
Axes of the slice: x: 4, y: 4, z: 16, core: 2. Of those that a mesh axis runs over, the one named last changes fastest.
Arguments:
- tokens: bfloat16 [32768, 2560], P('seq'), may hold values from -6 to 6
- w_query: bfloat16 [2560, 2560], P('seq', 'section'), may hold values from -0.125 to 0.125
- w_key: bfloat16 [2560, 2560], P('seq', 'section'), may hold values from -0.125 to 0.125
- w_value: bfloat16 [2560, 2560], P('seq', 'section'), may hold values from -0.125 to 0.125
- gain: bfloat16 [2560], P('section'), may hold values from 0.099609375 to 1.8984375
- w_out: bfloat16 [2560, 2560], P('section'), may hold values from -0.125 to 0.125
Outputs:
- hidden_out: bfloat16 [32768, 2560], P('seq', 'section')
All inputs are finite; a program needn't handle non-finite values.
Results may differ from a plain program's by a relative error of at most 0.015.
Values may be sent and summed in bfloat16 or wider, within the bound.
A program may use at most 128 MiB of HBM per device.

v0:
```python
import jax
import jax.numpy as jnp
from jax import lax
from jax.sharding import PartitionSpec as P

E = 128


def entering(value, axis, join, neutral):
    place = lax.axis_index(axis)
    gathered = lax.all_gather(value.astype(jnp.bfloat16), axis)
    state = jnp.zeros_like(value) + jnp.asarray(neutral, value.dtype)

    def one(step, state):
        return join(state, lax.dynamic_index_in_dim(gathered, step, 0, False).astype(value.dtype))

    return lax.fori_loop(0, place, one, state)


def add_states(earlier, later):
    return earlier + later


def carry_states(key_rows, value_rows, head_count):
    row_count = key_rows.shape[0]
    key_heads = key_rows.reshape(row_count, head_count, E)
    value_heads = value_rows.reshape(row_count, head_count, E)
    block_state = jnp.einsum(
        "chf,chg->hfg", key_heads, value_heads, preferred_element_type=jnp.float32
    )
    return entering(block_state, "seq", add_states, jnp.zeros_like(block_state))


def on_device(tokens, w_query, w_key, w_value, gain, w_out):
    row_count = tokens.shape[0]
    head_width = w_query.shape[1]
    head_count = head_width // E
    whole_query, whole_key, whole_value = (
        lax.all_gather(w_query, "seq", axis=0, tiled=True),
        lax.all_gather(w_key, "seq", axis=0, tiled=True),
        lax.all_gather(w_value, "seq", axis=0, tiled=True),
    )
    queries = jax.nn.silu(jnp.dot(tokens, whole_query, preferred_element_type=jnp.float32)).astype(
        jnp.bfloat16
    )
    key_rows = jax.nn.silu(jnp.dot(tokens, whole_key, preferred_element_type=jnp.float32)).astype(
        jnp.bfloat16
    )
    value_rows = jnp.dot(tokens, whole_value, preferred_element_type=jnp.float32).astype(
        jnp.bfloat16
    )
    earlier = carry_states(key_rows, value_rows, head_count)
    query_heads = queries.reshape(row_count, head_count, E)
    key_heads = key_rows.reshape(row_count, head_count, E)
    value_heads = value_rows.reshape(row_count, head_count, E)
    causal = jnp.arange(row_count)[:, None] >= jnp.arange(row_count)[None, :]
    scores = jnp.einsum("chf,dhf->hcd", query_heads, key_heads, preferred_element_type=jnp.float32)
    scores = jnp.where(causal[None], scores, 0.0).astype(jnp.bfloat16)
    local_part = jnp.einsum("hcd,dhf->chf", scores, value_heads, preferred_element_type=jnp.float32)
    carried = jnp.einsum(
        "chf,hfg->chg",
        query_heads,
        earlier.astype(jnp.bfloat16),
        preferred_element_type=jnp.float32,
    )
    combined = carried + local_part
    scale_rows = gain.astype(jnp.float32).reshape(head_count, E)
    normed = (
        combined
        * lax.rsqrt(jnp.mean(combined * combined, axis=-1, keepdims=True) + 1e-05)
        * scale_rows
    )
    attended = normed.reshape(row_count, head_width).astype(jnp.bfloat16)
    projected = jnp.dot(attended, w_out, preferred_element_type=jnp.float32)
    summed = lax.psum_scatter(
        projected.astype(jnp.bfloat16), "section", scatter_dimension=1, tiled=True
    ).astype(jnp.float32)
    quarter = summed.shape[1]
    own_columns = lax.dynamic_slice_in_dim(tokens, lax.axis_index("section") * quarter, quarter, 1)
    return (own_columns.astype(jnp.float32) + summed).astype(jnp.bfloat16)


def solution(mesh):
    placed = (
        P("seq", None),
        P("seq", "section"),
        P("seq", "section"),
        P("seq", "section"),
        P("section"),
        P("section", None),
    )
    return jax.shard_map(
        on_device, mesh=mesh, in_specs=placed, out_specs=P("seq", "section"), check_vma=False
    )
```

profile of v0, /device:TPU:1, one launch (start us, length us, event | category | flops | bytes accessed | tf_op | source)
XLA Modules:
  0.0 870.5 jit_solution(5385153539772552975)
XLA Ops:
  8.8 149.1 %all-gather.11.cloned.1.call-done = bf16[128,20,640]{2,1,0:T(8,128)(2,1)} async-done(((bf16[1,20,640]{2,1,0:T(8,128)(2,1)}), bf16[128,20,640]{2,1,0:T(8,128)(2,1)}) %all-gather.11.cloned.1.call-update) | async-done | bytes 3276816 | tf_op jit(solution)/shard_map/all_gather | solution.py:40
  157.9 6.1 reshape.43
  164.0 4.3 multiply_convert_fusion.2
  168.3 1.9 copy.18
  170.1 128.6 %all-gather.13.cloned.1.call-done = bf16[128,20,640]{2,1,0:T(8,128)(2,1)} async-done(((bf16[1,20,640]{2,1,0:T(8,128)(2,1)}), bf16[128,20,640]{2,1,0:T(8,128)(2,1)}) %all-gather.13.cloned.1.call-update) | async-done | bytes 3276816 | tf_op jit(solution)/shard_map/all_gather | solution.py:41
  298.7 6.1 reshape.45
  304.9 4.2 convolution_convert_fusion.1
  309.1 1.9 copy.19
  311.0 2.0 convolution_convert_fusion.2
  313.1 126.5 %all-gather.15.cloned.1.call-done = bf16[128,20,640]{2,1,0:T(8,128)(2,1)} async-done(((bf16[1,20,640]{2,1,0:T(8,128)(2,1)}), bf16[128,20,640]{2,1,0:T(8,128)(2,1)}) %all-gather.15.cloned.1.call-update) | async-done | bytes 3276816 | tf_op jit(solution)/shard_map/all_gather | solution.py:39
  439.6 6.1 reshape.47
  445.7 4.3 multiply_convert_fusion.1
  449.9 1.9 copy.21
  451.8 151.2 %all-gather.9.cloned.1.call-done = bf16[640,128,128]{2,1,0:T(8,128)(2,1)} async-done(((bf16[5,128,128]{2,1,0:T(8,128)(2,1)}), bf16[640,128,128]{2,1,0:T(8,128)(2,1)}) %all-gather.9.cloned.1.call-update) | async-done | bytes 20971536 | tf_op jit(solution)/shard_map/all_gather | solution.py:11
  603.8 1.8 while.10
  603.8 1.8 convert_add_fusion.2
  605.5 2.2 fusion.6
  607.8 2.8 multiply_reduce_fusion
  610.6 1.2 multiply_convert_fusion
  611.8 2.3 convolution_convert_fusion
  614.1 2.4 copy.31
  616.6 243.7 %reduce-scatter.4.cloned.1.call-done = bf16[640,256]{1,0:T(8,128)(2,1)} async-done(((bf16[2560,256]{1,0:T(8,128)(2,1)}), bf16[640,256]{1,0:T(8,128)(2,1)}) %reduce-scatter.4.cloned.1.call-update) | async-done | bytes 327696
  860.2 1.9 copy.32
  862.1 1.9 add_convert_fusion
  (18 shorter events, 3.1 us)
Async XLA Ops:
  6.5 605.3 %copy-start = (bf16[640,2560]{1,0:T(8,128)(2,1)S(1)}, bf16[640,2560]{1,0:T(8,128)(2,1)}, u32[]{:S(2)}) copy-start(bf16[640,2560]{1,0:T(8,128)(2,1)} %param.13) | copy-start | bytes 9830404
  6.5 151.4 %all-gather.11.cloned.1.call-start = ((), (), s32[]{:S(2)}) async-start(), calls=%async_computation.2 | async-start | bytes 3962880 | tf_op jit(solution)/shard_map/all_gather | solution.py:40
  7.3 291.5 %all-gather.13.cloned.1.call-start = ((), (), s32[]{:S(2)}) async-start(), calls=%async_computation.3 | async-start | bytes 3962880 | tf_op jit(solution)/shard_map/all_gather | solution.py:41
  8.0 431.6 %all-gather.15.cloned.1.call-start = ((), (), s32[]{:S(2)}) async-start(), calls=%async_computation.4 | async-start | bytes 3962880 | tf_op jit(solution)/shard_map/all_gather | solution.py:39
  8.7 594.3 %all-gather.9.cloned.1.call-start = ((), (), s32[]{:S(2)}) async-start(), calls=%async_computation.1 | async-start | bytes 21135360 | tf_op jit(solution)/shard_map/all_gather | solution.py:11
  304.9 8.2 copy-start.1
  313.0 547.3 %reduce-scatter.4.cloned.1.call-start = ((), (), s32[]{:S(2)}) async-start(), calls=%async_computation.5 | async-start | bytes 1638400
Sparse Core Ops, SparseCore 0:
  10.4 147.4 all-gather.10
  161.0 137.7 all-gather.12
  301.8 137.7 all-gather.14
  442.6 160.4 all-gather.8
  616.7 243.4 reduce-scatter.3
where the time goes:
time: 874 us; the launch traced here: 871 us
  waiting for transfers between devices  801 us (92%)
  local copies, waits for them, and re-layouts  29 us (3%)
  matrix products  22 us (3%)
  between operations  13.2 us (2%)
    unnamed x6, waiting for transfers between devices  246 us
    all_gather x1, waiting for transfers between devices, entering(): gathered = lax.all_gather(value.astype(jnp.bfloat16), axis)  151 us
    all_gather x1, waiting for transfers between devices, on_device(): lax.all_gather(w_key, 'seq', axis=0, tiled=True)  149 us
    all_gather x1, waiting for transfers between devices, on_device(): lax.all_gather(w_value, 'seq', axis=0, tiled=True)  129 us
    all_gather x1, waiting for transfers between devices, on_device(): lax.all_gather(w_query, 'seq', axis=0, tiled=True)  126 us
    unnamed x9, local copies, waits for them, and re-layouts  22.6 us
  transfers between devices with their start and end apart: 5, of which 5 were waited for; matrix products, arithmetic and copies ran while one was open for 4% of the time, Pallas kernels for 0%

commit v1 on v0

v1 whole, which is shorter than its diff:
```python
import jax
import jax.numpy as jnp
from jax import lax
from jax.experimental import pallas as pl
from jax.experimental.pallas import tpu as pltpu
from jax.sharding import PartitionSpec as P

E = 128
X, Z, Y = 4, 16, 4
HALF = Z // 2
ROWS = 20
HEADS = 5
COLS = 3 * HEADS
TILES = COLS + 4
CUT = 7
SPAN = 256
OWNERS, SHARE = 10, 2
MESH = pl.DeviceIdType.MESH
BF = jnp.bfloat16
F32 = jnp.float32


def dot(a, b):
    return jnp.dot(a, b, preferred_element_type=F32)


def kernel(
    tokens, wq, wk, wv, gain, w_out, out,
    G, T1, T2, PB, acc, wo, kvq, local, att,
    state, sib_state, chip_sum, zin, xout, xin, pout, pin, pfull,
    axs, axr, azs, azr, bzs, bzr, bxs, bxr, sas, sar, sbs, sbr,
    ws, wr, vs, vr, wl, ps, pr, z1s, z1r, xs, xr, z2s, z2r, qs, qr, ats, atr,
):
    seq = lax.axis_index("seq")
    y = lax.axis_index("section")
    c = lax.rem(seq, 2)
    z = lax.rem(lax.div(seq, 2), Z)
    x = lax.div(seq, 2 * Z)

    def at(dx=0, dy=0, dz=0, core=None):
        core = c if core is None else core
        nx, ny, nz = lax.rem(x + dx + X, X), lax.rem(y + dy + Y, Y), lax.rem(z + dz + Z, Z)
        return (ny, (nx * Z + nz) * 2 + core)

    def zz(d):
        return lax.rem(z + d + Z, Z)

    def rcopy(src, dst, ssem, rsem, dev):
        return pltpu.make_async_remote_copy(
            src_ref=src, dst_ref=dst, send_sem=ssem, recv_sem=rsem,
            device_id=dev, device_id_type=MESH,
        )

    sibling = at(core=1 - c)

    weights = (wk, wv, wq)
    for t in range(COLS):
        G[c, z, x, t] = weights[t // HEADS][0:16, pl.ds((t % HEADS) * E, E)]
    for u in range(4):
        parts = []
        for j in range(4):
            t = 4 * u + j
            if t < COLS:
                parts.append(weights[t // HEADS][16:20, pl.ds((t % HEADS) * E, E)].astype(F32))
            else:
                parts.append(jnp.zeros((4, E), F32))
        G[c, z, x, COLS + u] = jnp.concatenate(parts, axis=0).astype(BF)

    barrier = pltpu.get_barrier_semaphore()
    near = [at(dz=1), at(dz=-1), at(dx=1), at(dx=-1), at(dx=2), sibling, at(dy=1), at(dy=-1), at(dy=2)]
    for dev in near:
        pl.semaphore_signal(barrier, inc=1, device_id=dev, device_id_type=MESH)
    pl.semaphore_wait(barrier, len(near))

    XD = (1, -1, 2)

    def a_x(k):
        ref = G.at[c, z, x, pl.ds(0, CUT)]
        return rcopy(ref, ref, axs.at[k], axr.at[k], at(dx=XD[k]))

    def a_z(way, step, block, dz):
        ref = G.at[c, block, :, pl.ds(0, CUT)]
        return rcopy(ref, ref, azs.at[way, step], azr.at[way, step], at(dz=dz))

    def b_z(way, step, block, dz):
        ref = G.at[c, block, x, pl.ds(CUT, TILES - CUT)]
        return rcopy(ref, ref, bzs.at[way, step], bzr.at[way, step], at(dz=dz))

    def b_x(n, block, k):
        ref = G.at[c, block, x, pl.ds(CUT, TILES - CUT)]
        return rcopy(ref, ref, bxs.at[n, k], bxr.at[n, k], at(dx=XD[k]))

    def s_a(n, block):
        ref = G.at[c, block, :, pl.ds(0, CUT)]
        return rcopy(ref, ref, sas.at[n], sar.at[n], sibling)

    def s_b(n, block):
        ref = G.at[c, block, :, pl.ds(CUT, TILES - CUT)]
        return rcopy(ref, ref, sbs.at[n], sbr.at[n], sibling)

    def block_of(n):
        if n == 0:
            return z
        if n == Z - 1:
            return zz(HALF)
        return zz(-((n + 1) // 2)) if n % 2 else zz(n // 2)

    def blocks_at(step):
        return [0] if step == 0 else ([Z - 1] if step == HALF else [2 * step - 1, 2 * step])

    def w_y(k):
        dev = at(dy=XD[k])
        return rcopy(
            w_out.at[pl.ds(320 * c, 320), pl.ds(pl.multiple_of(640 * dev[0], 128), 640)],
            wo.at[y, pl.ds(320 * c, 320)], ws.at[k], wr.at[k], dev,
        )

    def w_s(k):
        ref = wo.at[lax.rem(y - XD[k] + Y, Y), pl.ds(320 * c, 320)]
        return rcopy(ref, ref, vs.at[k], vr.at[k], sibling)

    def w_own():
        return pltpu.make_async_copy(
            w_out.at[:, pl.ds(pl.multiple_of(640 * y, 128), 640)], wo.at[y], wl
        )

    for k in range(3):
        a_x(k).start()
    b_z(0, 0, z, 1).start()
    b_z(1, 0, z, -1).start()
    for k in range(3):
        b_x(0, z, k).start()
    for k in range(3):
        w_y(k).start()
    w_own().start()

    PB[...] = jnp.zeros_like(PB)
    row = lax.broadcasted_iota(jnp.int32, (80, 256), 0)
    lane = lax.broadcasted_iota(jnp.int32, (80, 256), 1)
    base = (lane >> 7) * 40 + ((lane >> 6) & 1) * 20
    r16 = lane & 15
    for xx in range(X):
        here = ((lane >> 4) & 3) == xx
        PB[0, xx, 176:256] = jnp.where(here & (row == base + r16), 1.0, 0.0).astype(BF)
        PB[1, xx, 176:256] = jnp.where(here & (row == base + 16 + (r16 & 3)), 1.0, 0.0).astype(BF)
    acc[...] = jnp.zeros_like(acc)

    lane_j = (lax.broadcasted_iota(jnp.int32, (SPAN, E), 1) & 15) >> 2

    def arrange(m, _):
        window = jnp.minimum(lax.div(80 * m, 128), 3)
        off = pl.multiple_of(176 - (80 * m - 128 * window), 16)
        lhs = jnp.concatenate(
            [tokens[:, pl.ds(pl.multiple_of(640 * xx + 128 * window, 128), 256)] for xx in range(X)], axis=1
        )
        first = dot(lhs, jnp.concatenate([PB[0, xx, pl.ds(off, 256)] for xx in range(X)], axis=0)).astype(BF)
        rest = dot(lhs, jnp.concatenate([PB[1, xx, pl.ds(off, 256)] for xx in range(X)], axis=0))
        for half in range(2):
            T1[2 * m + half] = first[:, half * E:(half + 1) * E]
            part = rest[:, half * E:(half + 1) * E]
            for j in range(4):
                T2[j, 2 * m + half] = jnp.where(lane_j == j, part, 0.0).astype(BF)
        return 0

    lax.fori_loop(0, Z // 2, arrange, 0)

    def multiply(z1, z2):
        def pair(p, _):
            h, j = lax.div(p, 4), lax.rem(p, 4)
            lhs = jnp.concatenate([T1[z1], T1[z2], T2[j, z1], T2[j, z2]], axis=1)

            def block(t):
                return jnp.concatenate([G[:, z1, :, t].reshape(E, E), G[:, z2, :, t].reshape(E, E)], axis=0)

            t1, t2 = 8 * h + j, 8 * h + 4 + j
            u1, u2 = COLS + 2 * h, COLS + 2 * h + 1
            rhs = jnp.concatenate(
                [jnp.concatenate([block(t1), block(t2)], axis=1), jnp.concatenate([block(u1), block(u2)], axis=1)],
                axis=0,
            )
            acc[p] += dot(lhs, rhs)
            return 0

        lax.fori_loop(0, 8, pair, 0)

    def sibling_b(step):
        for n in blocks_at(step):
            for k in range(3):
                b_x(n, block_of(n), k).wait_recv()
            s_b(n, block_of(n)).start()

    def consume(step):
        for n in blocks_at(step):
            s_a(n, block_of(n)).wait_recv()
            s_b(n, block_of(n)).wait_recv()

    def multiply_step(step):
        consume(step)
        if step == HALF:
            multiply(z, zz(HALF))
        elif step > 0:
            multiply(zz(-step), zz(step))

    for k in range(3):
        a_x(k).wait_recv()
    a_z(0, 0, z, 1).start()
    a_z(1, 0, z, -1).start()
    s_a(0, z).start()

    way = 1 - 2 * c
    for step in range(1, HALF):
        last = step == HALF - 1
        minus, plus = zz(-step), zz(step)
        b_z(0, step - 1, minus, 1).wait_recv()
        if not last:
            b_z(0, step, minus, 1).start()
        b_z(1, step - 1, plus, -1).wait_recv()
        if not last:
            b_z(1, step, plus, -1).start()
        else:
            b_z(c, step, zz(-step * way), way).start()
        for n, block in zip(blocks_at(step), (minus, plus)):
            for k in range(3):
                b_x(n, block, k).start()
        a_z(0, step - 1, minus, 1).wait_recv()
        if not last:
            a_z(0, step, minus, 1).start()
        a_z(1, step - 1, plus, -1).wait_recv()
        if not last:
            a_z(1, step, plus, -1).start()
        else:
            a_z(c, step, zz(-step * way), way).start()
        for n, block in zip(blocks_at(step), (minus, plus)):
            s_a(n, block).start()
        sibling_b(step - 1)
        if step >= 2:
            multiply_step(step - 2)
        if step == 4:
            for k in range(3):
                w_y(k).wait_recv()
                w_s(k).start()
            w_own().wait()

    far = zz(HALF)
    b_z(c, HALF - 1, far, way).wait_recv()
    for k in range(3):
        b_x(Z - 1, far, k).start()
    a_z(c, HALF - 1, far, way).wait_recv()
    s_a(Z - 1, far).start()
    sibling_b(HALF - 1)
    multiply_step(HALF - 2)
    sibling_b(HALF)
    multiply_step(HALF - 1)
    multiply_step(HALF)

    def tile(t):
        p, half = (t // 8) * 4 + t % 4, (t % 8) // 4
        return acc[p, :, half * E:(half + 1) * E]

    def silu(v):
        return v / (1.0 + jnp.exp(-v))

    for h in range(HEADS):
        kvq[h] = silu(tile(h)).astype(BF)
        kvq[HEADS + h] = tile(HEADS + h).astype(BF)
        s = lax.dot_general(kvq[h], kvq[HEADS + h], (((0,), (0,)), ((), ())), preferred_element_type=F32)
        state[pl.ds(8 * h, 8)] = s.astype(BF).reshape(8, 16, E)
    pair1 = rcopy(state, sib_state, ps, pr, sibling)
    pair1.start()
    for h in range(HEADS):
        kvq[2 * HEADS + h] = silu(tile(2 * HEADS + h)).astype(BF)
    pair1.wait_recv()
    mine = pl.ds(20 * c, 20)
    chip_sum[...] = (state[mine].astype(F32) + sib_state[mine].astype(F32)).astype(BF)

    def owner_z(i):
        return (i * Z) // OWNERS

    def z1(i):
        dst = owner_z(i)
        return rcopy(
            chip_sum.at[pl.ds(SHARE * i, SHARE)], zin.at[z], z1s.at[i], z1r.at[z],
            (y, (x * Z + dst) * 2 + c),
        )

    my_i = lax.div(z * OWNERS + Z - 1, Z)
    is_owner = lax.div(my_i * Z, OWNERS) == z
    for i in range(OWNERS):
        @pl.when(z != owner_z(i))
        def _():
            z1(i).start()

        @pl.when(z == owner_z(i))
        def _():
            zin[z] = chip_sum[pl.ds(SHARE * i, SHARE)]

    causal = lax.broadcasted_iota(jnp.int32, (SPAN, SPAN), 0) >= lax.broadcasted_iota(jnp.int32, (SPAN, SPAN), 1)
    for h in range(HEADS):
        q, k, v = kvq[2 * HEADS + h], kvq[h], kvq[HEADS + h]
        scores = lax.dot_general(q, k, (((1,), (1,)), ((), ())), preferred_element_type=F32)
        local[h] = dot(jnp.where(causal, scores, 0.0).astype(BF), v)

    def x_copy(k):
        return rcopy(xout, xin.at[x], xs.at[k], xr.at[k], at(dx=XD[k]))

    def z1_in(src):
        return rcopy(chip_sum.at[pl.ds(0, SHARE)], zin.at[src], z1s.at[0], z1r.at[src], sibling)

    def z2(dst):
        return rcopy(
            pout.at[dst], pin.at[pl.ds(SHARE * my_i, SHARE)], z2s.at[dst], z2r.at[my_i],
            (y, (x * Z + dst) * 2 + c),
        )

    def z2_in(i):
        return rcopy(pout.at[0], pin.at[pl.ds(SHARE * i, SHARE)], z2s.at[0], z2r.at[i], sibling)

    @pl.when(is_owner)
    def _():
        for src in range(Z):
            @pl.when(src != z)
            def _():
                z1_in(src).wait_recv()
        total = jnp.zeros((SHARE, 16, E), F32)
        for src in range(Z):
            total = total + zin[src].astype(F32)
        xout[...] = total
        for k in range(3):
            x_copy(k).start()
        for k in range(3):
            x_copy(k).wait_recv()
        running = jnp.zeros((SHARE, 16, E), F32)
        for src in range(X):
            running = running + jnp.where((src < x), xin[src], 0.0)
        for dst in range(Z):
            pout[dst] = running.astype(BF)
            running = running + zin[dst].astype(F32)

            @pl.when(dst != z)
            def _():
                z2(dst).start()
        pin[pl.ds(SHARE * my_i, SHARE)] = pout[z]

    for i in range(OWNERS):
        @pl.when(z != owner_z(i))
        def _():
            z2_in(i).wait_recv()
    pair2 = rcopy(pin, pfull.at[pl.ds(20 * c, 20)], qs, qr, sibling)
    pair2.start()
    pfull[mine] = pin[...]
    pair2.wait_recv()

    def a_y(k, h):
        return rcopy(att.at[y, h], att.at[y, h], ats.at[k, h], atr.at[k, h], at(dy=XD[k]))

    for h in range(HEADS):
        before = pfull[pl.ds(8 * h, 8)].reshape(E, E).astype(F32)
        first = sib_state[pl.ds(8 * h, 8)].reshape(E, E).astype(F32)
        prefix = jnp.where(c == 1, before + first, before).astype(BF)
        combined = dot(kvq[2 * HEADS + h], prefix) + local[h]
        scale = lax.rsqrt(jnp.mean(combined * combined, axis=-1, keepdims=True) + 1e-05)
        att[y, h] = (combined * scale * gain[h:h + 1].astype(F32)).astype(BF)
        for k in range(3):
            a_y(k, h).start()

    def project(section):
        lhs = jnp.concatenate([att[section, h] for h in range(HEADS)], axis=1)
        return dot(lhs, wo[section])

    for k in range(3):
        w_s(k).wait_recv()
    total = tokens[:, pl.ds(pl.multiple_of(640 * y, 128), 640)].astype(F32) + project(y)

    for k in range(3):
        a_x(k).wait_send()
        w_y(k).wait_send()
        w_s(k).wait_send()
    for step in range(HALF - 1):
        for w, dz in ((0, 1), (1, -1)):
            a_z(w, step, z, dz).wait_send()
            b_z(w, step, z, dz).wait_send()
    a_z(c, HALF - 1, z, way).wait_send()
    b_z(c, HALF - 1, z, way).wait_send()
    for n in range(Z):
        s_a(n, z).wait_send()
        s_b(n, z).wait_send()
        for k in range(3):
            b_x(n, z, k).wait_send()
    pair1.wait_send()
    pair2.wait_send()
    for i in range(OWNERS):
        @pl.when(z != owner_z(i))
        def _():
            z1(i).wait_send()

    @pl.when(is_owner)
    def _():
        for k in range(3):
            x_copy(k).wait_send()
        for dst in range(Z):
            @pl.when(dst != z)
            def _():
                z2(dst).wait_send()

    for k in range(3):
        for h in range(HEADS):
            a_y(k, h).wait_recv()
        total = total + project(lax.rem(y - XD[k] + Y, Y))
    out[...] = total.astype(BF)
    for k in range(3):
        for h in range(HEADS):
            a_y(k, h).wait_send()


def on_device(tokens, w_query, w_key, w_value, gain, w_out):
    vmem = pl.BlockSpec(memory_space=pltpu.VMEM)
    dma = pltpu.SemaphoreType.DMA
    return pl.pallas_call(
        kernel,
        name="layer",
        out_shape=jax.ShapeDtypeStruct((SPAN, 640), BF),
        in_specs=[vmem, vmem, vmem, vmem, vmem, pl.BlockSpec(memory_space=pl.ANY)],
        out_specs=vmem,
        scratch_shapes=[
            pltpu.VMEM((2, Z, X, TILES, 16, E), BF),
            pltpu.VMEM((Z, SPAN, E), BF),
            pltpu.VMEM((4, Z, SPAN, E), BF),
            pltpu.VMEM((2, X, 432, 256), BF),
            pltpu.VMEM((8, SPAN, 256), F32),
            pltpu.VMEM((Y, 640, 640), BF),
            pltpu.VMEM((COLS, SPAN, E), BF),
            pltpu.VMEM((HEADS, SPAN, E), F32),
            pltpu.VMEM((Y, HEADS, SPAN, E), BF),
            pltpu.VMEM((40, 16, E), BF),
            pltpu.VMEM((40, 16, E), BF),
            pltpu.VMEM((20, 16, E), BF),
            pltpu.VMEM((Z, SHARE, 16, E), BF),
            pltpu.VMEM((SHARE, 16, E), F32),
            pltpu.VMEM((X, SHARE, 16, E), F32),
            pltpu.VMEM((Z, SHARE, 16, E), BF),
            pltpu.VMEM((20, 16, E), BF),
            pltpu.VMEM((40, 16, E), BF),
            dma((3,)), dma((3,)),
            dma((2, HALF)), dma((2, HALF)),
            dma((2, HALF)), dma((2, HALF)),
            dma((Z, 3)), dma((Z, 3)),
            dma((Z,)), dma((Z,)), dma((Z,)), dma((Z,)),
            dma((3,)), dma((3,)), dma((3,)), dma((3,)), dma(()),
            dma(()), dma(()),
            dma((OWNERS,)), dma((Z,)),
            dma((3,)), dma((3,)),
            dma((Z,)), dma((OWNERS,)),
            dma(()), dma(()),
            dma((3, HEADS)), dma((3, HEADS)),
        ],
        compiler_params=pltpu.CompilerParams(
            collective_id=1, has_side_effects=True, vmem_limit_bytes=56 << 20
        ),
    )(tokens, w_query, w_key, w_value, gain.reshape(HEADS, E), w_out)


def solution(mesh):
    placed = (
        P("seq", None),
        P("seq", "section"),
        P("seq", "section"),
        P("seq", "section"),
        P("section"),
        P("section", None),
    )
    return jax.shard_map(
        on_device, mesh=mesh, in_specs=placed, out_specs=P("seq", "section"), check_vma=False
    )
```

time: 874 us -> 108 us (0.12)
  waiting for transfers between devices: 801 us -> 0 us
  Pallas kernels: 0 us -> 106 us
  local copies, waits for them, and re-layouts: 29 us -> 1.73 us
  matrix products: 22 us -> 0 us
  between operations: 13.2 us -> 0.01 us
    all_gather x4 -> x0, waiting for transfers between devices: 555 us -> none  [the longest x1 151 us: entering(): gathered = lax.all_gather(value.astype(jnp.bfloat16), axis)]
    unnamed x6 -> x0, waiting for transfers between devices: 246 us -> none
    pallas_call x0 -> x1, Pallas kernels: none -> 106 us  [on_device(): pl.pallas_call(kernel, name='layer', out_shape=jax.ShapeDtypeStruct((SPAN...]
    dot_general x7 -> x0, matrix products: 22 us -> none  [the longest x1 4.25 us: on_device(): jnp.dot(tokens, whole_key, preferred_element_type=jnp.float32)]
    unnamed x9 -> x1, local copies, waits for them, and re-layouts: 22.6 us -> 1.73 us
  transfers between devices with their start and end apart: 5 -> 0, of which waited for: 5 -> 0; matrix products, arithmetic and copies ran while one was open for 4% -> 0% of each run, Pallas kernels for 0% -> 0%
where the time goes in v1:
time: 108 us
  Pallas kernels  106 us (98%)
  local copies, waits for them, and re-layouts  1.73 us (2%)
    pallas_call x1, Pallas kernels, on_device(): pl.pallas_call(kernel, name='layer', out_shape=jax.ShapeDtypeStruct((SPAN...  106 us

profile of v1, /device:TPU:1, one launch (start us, length us, event | category | flops | bytes accessed | tf_op | source)
XLA Modules:
  0.0 107.8 jit_solution(5352751189747732711)
XLA Ops:
  0.0 106.1 %layer.1 = bf16[256,640]{1,0:T(8,128)(2,1)} custom-call(bf16[256,2560]{1,0:T(8,128)(2,1)} %tokens.1, bf16[20,640]{1,0:T(8,128)(2,1)} %wq.1, bf16[20,640]{1,0:T(8,128)(2,1)} %wk.1, bf16[20,640]{1,0:T(8,128)(2,1)} %wv.1, bf16[5,128]{1,0:T(8,128)(2,1)} %bitcast.1, bf16[640,2560]{1,0:T(8,128)(2,1)} %w_out.1), custom_call_target="tpu_custom_call" | custom-call | tf_op jit(solution)/shard_map/layer/pallas_call | solution.py:418
  106.1 1.7 %copy.8 = bf16[256,640]{1,0:T(8,128)(2,1)} copy(bf16[256,640]{1,0:T(8,128)(2,1)} %layer.1) | data formatting | bytes 655360

commit v2 on v1

v2 whole, which is shorter than its diff:
```python
import jax
import jax.numpy as jnp
from jax import lax
from jax.experimental import pallas as pl
from jax.experimental.pallas import tpu as pltpu
from jax.sharding import PartitionSpec as P

E = 128
X, Z, Y = 4, 16, 4
ROWS = 20
HEADS = 5
COLS = 3 * HEADS
FIRST = (0, 2 * HEADS)
WIDE = (2 * HEADS, HEADS)
TILES = (13, 7)
CUT = (3, 2)
SPAN = 256
OWNERS, SHARE = 10, 2
MESH = pl.DeviceIdType.MESH
BF = jnp.bfloat16
F32 = jnp.float32


def dot(a, b):
    return jnp.dot(a, b, preferred_element_type=F32)


def kernel(
    tokens_hbm, wq, wk, wv, gain, w_out, out, tokens,
    G0, G1, T1, T2, PB, acc, wo, kvq, local, att,
    state, sib_state, chip_sum, zin, xout, xin, pout, pin, pfull,
    axs, axr, azs, azr, bzs, bzr, bxs, bxr, ss, sr,
    ws, wr, vs, vr, wl, ps, pr, z1s, z1r, xs, xr, z2s, z2r, qs, qr, ats, atr, tl,
):
    seq = lax.axis_index("seq")
    y = lax.axis_index("section")
    c = lax.rem(seq, 2)
    z = lax.rem(lax.div(seq, 2), Z)
    x = lax.div(seq, 2 * Z)

    def at(dx=0, dy=0, dz=0, core=None):
        core = c if core is None else core
        nx, ny, nz = lax.rem(x + dx + X, X), lax.rem(y + dy + Y, Y), lax.rem(z + dz + Z, Z)
        return (ny, (nx * Z + nz) * 2 + core)

    def zz(d):
        return lax.rem(z + d + Z, Z)

    def rcopy(src, dst, ssem, rsem, dev):
        return pltpu.make_async_remote_copy(
            src_ref=src, dst_ref=dst, send_sem=ssem, recv_sem=rsem,
            device_id=dev, device_id_type=MESH,
        )

    sibling = at(core=1 - c)

    way = 1 - 2 * c
    G = (G0, G1)

    barrier = pltpu.get_barrier_semaphore()
    greeted = [at(dz=d) for d in (1, -1, 2, -2, 3, -3)] + [at(dx=1), at(dx=-1), at(dx=2), sibling]
    greeted += [at(dy=1), at(dy=-1), at(dy=2)]
    for dev in greeted:
        pl.semaphore_signal(barrier, inc=1, device_id=dev, device_id_type=MESH)
    fetch = pltpu.make_async_copy(tokens_hbm, tokens, tl)
    fetch.start()

    weights = (wk, wv, wq)
    for ph in range(2):
        for i in range(WIDE[ph]):
            t = FIRST[ph] + i
            G[ph][c, z, x, i] = weights[t // HEADS][0:16, pl.ds((t % HEADS) * E, E)]
        for u in range(TILES[ph] - WIDE[ph]):
            parts = []
            for i in range(4 * u, 4 * u + 4):
                t = FIRST[ph] + i
                if i < WIDE[ph]:
                    parts.append(weights[t // HEADS][16:20, pl.ds((t % HEADS) * E, E)].astype(F32))
                else:
                    parts.append(jnp.zeros((4, E), F32))
            G[ph][c, z, x, WIDE[ph] + u] = jnp.concatenate(parts, axis=0).astype(BF)

    pl.semaphore_wait(barrier, len(greeted))

    XD = (1, -1, 2)

    def place(d):
        return (d + 7) % Z

    def part_a(ph):
        return pl.ds(0, CUT[ph])

    def part_b(ph):
        return pl.ds(CUT[ph], TILES[ph] - CUT[ph])

    def a_x(ph, k):
        ref = G[ph].at[c, z, x, part_a(ph)]
        return rcopy(ref, ref, axs.at[ph], axr.at[ph], at(dx=XD[k]))

    def a_x_in(ph):
        ref = G[ph].at[c, z, pl.ds(0, 3), part_a(ph)]
        return rcopy(ref, ref, axs.at[ph], axr.at[ph], sibling)

    def a_z(ph, d, delta):
        ref = G[ph].at[c, zz(d), :, part_a(ph)]
        return rcopy(ref, ref, azs.at[ph], azr.at[ph, place(d - delta)], at(dz=delta))

    def b_z(ph, d, delta):
        ref = G[ph].at[c, zz(d), x, part_b(ph)]
        return rcopy(ref, ref, bzs.at[ph], bzr.at[ph, place(d - delta)], at(dz=delta))

    def opposite(copy_of, ph):
        ref = copy_of(ph, zz(-6 * way))
        sems = (azs, azr) if copy_of is ref_a else (bzs, bzr)
        return rcopy(ref, ref, sems[0].at[ph], sems[1].at[ph, place(8)], at(dz=2 * way))

    def ref_a(ph, block):
        return G[ph].at[c, block, :, part_a(ph)]

    def ref_b(ph, block):
        return G[ph].at[c, block, x, part_b(ph)]

    def late(d):
        return abs(d) in (5, 7, 8)

    def b_x(ph, d, k):
        ref = ref_b(ph, zz(d))
        kind = 1 if late(d) else (c if k == 0 else 1 - c)
        return rcopy(ref, ref, bxs.at[ph], bxr.at[ph, place(d), kind], at(dx=XD[k]))

    def b_x_on(ph, d):
        ref = G[ph].at[c, zz(d), lax.rem(x - way + X, X), part_b(ph)]
        return rcopy(ref, ref, bxs.at[ph], bxr.at[ph, place(d), 1], at(dx=way))

    def b_x_in(ph, d, kind, count):
        ref = G[ph].at[c, zz(d), pl.ds(0, count), part_b(ph)]
        return rcopy(ref, ref, bxs.at[ph], bxr.at[ph, place(d), kind], sibling)

    def to_sibling(ph, d):
        ref = G[ph].at[c, zz(d)]
        return rcopy(ref, ref, ss.at[ph], sr.at[ph, place(d)], sibling)

    def onward(ph, d, copy, ref_of):
        if d == 0:
            for delta in (3, -3, 1, -1):
                copy(ph, 0, delta).start()
        if abs(d) == 3:
            for delta in (-d, -d // 3, d // 3):
                copy(ph, d, delta).start()
        if abs(d) == 6:
            for delta in (-d // 6, d // 6):
                copy(ph, d, delta).start()

    def A(ph, *ds):
        for d in ds:
            ref = ref_a(ph, zz(d))
            rcopy(ref, ref, azs.at[ph], azr.at[ph, place(d)], sibling).wait_recv()
            onward(ph, d, a_z, ref_a)
        if 6 in ds:
            opposite(ref_a, ph).start()

    def B(ph, *ds):
        for d in ds:
            ref = ref_b(ph, zz(d))
            rcopy(ref, ref, bzs.at[ph], bzr.at[ph, place(d)], sibling).wait_recv()
            onward(ph, d, b_z, ref_b)
        if 6 in ds:
            opposite(ref_b, ph).start()
        for d in ds:
            for k in range(3 if late(d) else 2):
                b_x(ph, d, k).start()

    def F(ph, *ds):
        for d in ds:
            b_x_in(ph, d, 0, 1).wait_recv()
            b_x_on(ph, d).start()

    def S(ph, *ds):
        for d in ds:
            b_x_in(ph, d, 1, 3 if late(d) else 2).wait_recv()
            to_sibling(ph, d).start()

    def AX(ph):
        a_x_in(ph).wait_recv()
        onward(ph, 0, a_z, ref_a)

    def w_y(k):
        dev = at(dy=XD[k])
        return rcopy(
            w_out.at[pl.ds(320 * c, 320), pl.ds(pl.multiple_of(640 * dev[0], 128), 640)],
            wo.at[y, pl.ds(320 * c, 320)], ws.at[k], wr.at[k], dev,
        )

    def w_s(k):
        ref = wo.at[lax.rem(y - XD[k] + Y, Y), pl.ds(320 * c, 320)]
        return rcopy(ref, ref, vs.at[k], vr.at[k], sibling)

    def w_own():
        return pltpu.make_async_copy(
            w_out.at[:, pl.ds(pl.multiple_of(640 * y, 128), 640)], wo.at[y], wl
        )

    def begin(ph):
        onward(ph, 0, b_z, ref_b)
        for k in range(2):
            b_x(ph, 0, k).start()

    for k in range(3):
        a_x(0, k).start()
    begin(0)
    for k in range(3):
        a_x(1, k).start()
    for k in range(3):
        w_y(k).start()
    w_own().start()

    PB[...] = jnp.zeros_like(PB)
    acc[...] = jnp.zeros_like(acc)
    row = lax.broadcasted_iota(jnp.int32, (80, 256), 0)
    lane = lax.broadcasted_iota(jnp.int32, (80, 256), 1)
    base = (lane >> 7) * 40 + ((lane >> 6) & 1) * 20
    r16 = lane & 15
    for xx in range(X):
        here = ((lane >> 4) & 3) == xx
        PB[0, xx, 176:256] = jnp.where(here & (row == base + r16), 1.0, 0.0).astype(BF)
        PB[1, xx, 176:256] = jnp.where(here & (row == base + 16 + (r16 & 3)), 1.0, 0.0).astype(BF)

    fetch.wait()
    lane_j = (lax.broadcasted_iota(jnp.int32, (SPAN, E), 1) & 15) >> 2

    def arrange(m, _):
        window = jnp.minimum(lax.div(80 * m, 128), 3)
        off = pl.multiple_of(176 - (80 * m - 128 * window), 16)
        lhs = jnp.concatenate(
            [tokens[:, pl.ds(pl.multiple_of(640 * xx + 128 * window, 128), 256)] for xx in range(X)], axis=1
        )
        first = dot(lhs, jnp.concatenate([PB[0, xx, pl.ds(off, 256)] for xx in range(X)], axis=0)).astype(BF)
        rest = dot(lhs, jnp.concatenate([PB[1, xx, pl.ds(off, 256)] for xx in range(X)], axis=0))
        for half in range(2):
            T1[2 * m + half] = first[:, half * E:(half + 1) * E]
            part = rest[:, half * E:(half + 1) * E]
            for j in range(4):
                T2[j, 2 * m + half] = jnp.where(lane_j == j, part, 0.0).astype(BF)
        return 0

    lax.fori_loop(0, Z // 2, arrange, 0, unroll=2)

    def M(ph, *ds):
        at_z = [zz(d) for d in ds]
        for d in ds:
            to_sibling(ph, d).wait_recv()

        def column(t):
            return jnp.concatenate([G[ph][:, b, :, t].reshape(E, E) for b in at_z], axis=0)

        def rows(j):
            return jnp.concatenate([T1[b] for b in at_z] + [T2[j, b] for b in at_z], axis=1)

        for i in range(WIDE[ph]):
            u, j, t = i // 4, i % 4, FIRST[ph] + i
            if u == 0 and i + 4 < min(WIDE[ph], 8):
                top = jnp.concatenate([column(i), column(i + 4)], axis=1)
                low = jnp.concatenate([column(WIDE[ph]), column(WIDE[ph] + 1)], axis=1)
                both = dot(rows(j), jnp.concatenate([top, low], axis=0))
                acc[t] += both[:, :E]
                acc[t + 4] += both[:, E:]
            elif u != 1:
                acc[t] += dot(rows(j), jnp.concatenate([column(i), column(WIDE[ph] + u)], axis=0))

    AX(0)
    B(0, 1, -1)
    B(0, 3, -3)
    F(0, 0)
    A(0, 1, -1)
    F(0, 1, -1)
    A(0, 3, -3)
    F(0, 3, -3)
    S(0, 0, 1, -1)
    B(0, 6, -6)
    B(0, 2, -2, 4, -4)
    S(0, 3, -3)
    M(0, 1, -1, 3, -3)
    A(0, 6, -6)
    F(0, 6, -6)
    F(0, 2, -2, 4, -4)
    A(0, 2, -2, 4, -4)
    B(0, 5, -5, 7, -7, 8)
    S(0, 2, -2, 4, -4)
    M(0, 2, -2, 4, -4)
    S(0, 6, -6)
    A(0, 5, -5, 7, -7, 8)
    begin(1)
    AX(1)
    M(0, 0, 6, -6)
    S(0, 5, -5)
    S(0, 7, -7, 8)
    M(0, 5, -5, 7, -7, 8)

    def tile(t):
        return acc[t]

    def silu(v):
        return v / (1.0 + jnp.exp(-v))

    for h in range(HEADS):
        kvq[h] = silu(tile(h)).astype(BF)
        kvq[HEADS + h] = tile(HEADS + h).astype(BF)
        s = lax.dot_general(kvq[h], kvq[HEADS + h], (((0,), (0,)), ((), ())), preferred_element_type=F32)
        state[pl.ds(8 * h, 8)] = s.astype(BF).reshape(8, 16, E)
    pair1 = rcopy(state, sib_state, ps, pr, sibling)
    pair1.start()
    B(1, 1, -1, 3, -3)
    pair1.wait_recv()
    mine = pl.ds(20 * c, 20)
    chip_sum[...] = (state[mine].astype(F32) + sib_state[mine].astype(F32)).astype(BF)

    def owner_z(i):
        return (i * Z) // OWNERS

    def z1(i):
        dst = owner_z(i)
        return rcopy(
            chip_sum.at[pl.ds(SHARE * i, SHARE)], zin.at[z], z1s.at[i], z1r.at[z],
            (y, (x * Z + dst) * 2 + c),
        )

    my_i = lax.div(z * OWNERS + Z - 1, Z)
    is_owner = lax.div(my_i * Z, OWNERS) == z
    for i in range(OWNERS):
        @pl.when(z != owner_z(i))
        def _():
            z1(i).start()

        @pl.when(z == owner_z(i))
        def _():
            zin[z] = chip_sum[pl.ds(SHARE * i, SHARE)]

    F(1, 0)
    A(1, 1, -1, 3, -3)
    F(1, 1, -1, 3, -3)
    B(1, 6, -6, 2, -2, 4, -4)
    S(1, 0, 1, -1, 3, -3)
    M(1, 1, -1, 3, -3)

    def x_copy(k):
        return rcopy(xout, xin.at[x], xs.at[k], xr.at[k], at(dx=XD[k]))

    def z1_in(src):
        return rcopy(chip_sum.at[pl.ds(0, SHARE)], zin.at[src], z1s.at[0], z1r.at[src], sibling)

    def z2(dst):
        return rcopy(
            pout.at[dst], pin.at[pl.ds(SHARE * my_i, SHARE)], z2s.at[dst], z2r.at[my_i],
            (y, (x * Z + dst) * 2 + c),
        )

    def z2_in(i):
        return rcopy(pout.at[0], pin.at[pl.ds(SHARE * i, SHARE)], z2s.at[0], z2r.at[i], sibling)

    @pl.when(is_owner)
    def _():
        for src in range(Z):
            @pl.when(src != z)
            def _():
                z1_in(src).wait_recv()
        total = jnp.zeros((SHARE, 16, E), F32)
        for src in range(Z):
            total = total + zin[src].astype(F32)
        xout[...] = total
        for k in range(3):
            x_copy(k).start()

    F(1, 6, -6, 2, -2, 4, -4)
    A(1, 6, -6, 2, -2, 4, -4)
    B(1, 5, -5, 7, -7, 8)
    S(1, 2, -2, 4, -4)

    @pl.when(is_owner)
    def _():
        for k in range(3):
            x_copy(k).wait_recv()
        running = jnp.zeros((SHARE, 16, E), F32)
        for src in range(X):
            running = running + jnp.where((src < x), xin[src], 0.0)
        for dst in range(Z):
            pout[dst] = running.astype(BF)
            running = running + zin[dst].astype(F32)

            @pl.when(dst != z)
            def _():
                z2(dst).start()
        pin[pl.ds(SHARE * my_i, SHARE)] = pout[z]

    M(1, 2, -2, 4, -4)
    S(1, 6, -6)
    A(1, 5, -5, 7, -7, 8)
    M(1, 0, 6, -6)
    S(1, 5, -5, 7, -7, 8)
    M(1, 5, -5, 7, -7, 8)
    for k in range(3):
        w_y(k).wait_recv()
        w_s(k).start()
    w_own().wait()
    for h in range(HEADS):
        kvq[2 * HEADS + h] = silu(tile(2 * HEADS + h)).astype(BF)
    causal = lax.broadcasted_iota(jnp.int32, (SPAN, SPAN), 0) >= lax.broadcasted_iota(jnp.int32, (SPAN, SPAN), 1)
    for h in range(HEADS):
        q, k, v = kvq[2 * HEADS + h], kvq[h], kvq[HEADS + h]
        scores = lax.dot_general(q, k, (((1,), (1,)), ((), ())), preferred_element_type=F32)
        local[h] = dot(jnp.where(causal, scores, 0.0).astype(BF), v)

    for i in range(OWNERS):
        @pl.when(z != owner_z(i))
        def _():
            z2_in(i).wait_recv()
    pair2 = rcopy(pin, pfull.at[pl.ds(20 * c, 20)], qs, qr, sibling)
    pair2.start()
    pfull[mine] = pin[...]
    pair2.wait_recv()

    def a_y(k, h):
        ref = att.at[y, h]
        return rcopy(ref, ref, ats.at[k], atr.at[c if k == 0 else 1 - c, h], at(dy=XD[k]))

    def a_y_on(h):
        ref = att.at[lax.rem(y - way + Y, Y), h]
        return rcopy(ref, ref, ats.at[2], atr.at[2, h], at(dy=way))

    def a_y_in(kind, h):
        return rcopy(att.at[y, h], att.at[y, h], ats.at[0], atr.at[kind, h], sibling)

    for h in range(HEADS):
        before = pfull[pl.ds(8 * h, 8)].reshape(E, E).astype(F32)
        first = sib_state[pl.ds(8 * h, 8)].reshape(E, E).astype(F32)
        prefix = jnp.where(c == 1, before + first, before).astype(BF)
        combined = dot(kvq[2 * HEADS + h], prefix) + local[h]
        scale = lax.rsqrt(jnp.mean(combined * combined, axis=-1, keepdims=True) + 1e-05)
        att[y, h] = (combined * scale * gain[h:h + 1].astype(F32)).astype(BF)
        for k in range(2):
            a_y(k, h).start()

    def project(section):
        lhs = jnp.concatenate([att[section, h] for h in range(HEADS)], axis=1)
        return dot(lhs, wo[section])

    for k in range(3):
        w_s(k).wait_recv()
    total = tokens[:, pl.ds(pl.multiple_of(640 * y, 128), 640)].astype(F32) + project(y)
    for h in range(HEADS):
        a_y_in(0, h).wait_recv()
        a_y_on(h).start()
    total = total + project(lax.rem(y - way + Y, Y))

    for k in range(3):
        w_y(k).wait_send()
        w_s(k).wait_send()

    def sent(ref, sem):
        rcopy(ref, ref, sem, sem, sibling).wait_send()

    for ph in range(2):
        sent(G[ph].at[c, z, pl.ds(0, 3), part_a(ph)], axs.at[ph])
        sent(G[ph].at[c, pl.ds(0, Z - 1), :, part_a(ph)], azs.at[ph])
        sent(G[ph].at[c, pl.ds(0, Z - 1), x, part_b(ph)], bzs.at[ph])
        sent(G[ph].at[c, :, pl.ds(0, 3), part_b(ph)], bxs.at[ph])
        sent(G[ph].at[c], ss.at[ph])
    pair1.wait_send()
    pair2.wait_send()
    for i in range(OWNERS):
        @pl.when(z != owner_z(i))
        def _():
            z1(i).wait_send()

    @pl.when(is_owner)
    def _():
        for k in range(3):
            x_copy(k).wait_send()
        for dst in range(Z):
            @pl.when(dst != z)
            def _():
                z2(dst).wait_send()

    for kind, section in ((1, y + way), (2, y + 2)):
        for h in range(HEADS):
            a_y_in(kind, h).wait_recv()
        total = total + project(lax.rem(section + Y, Y))
    out[...] = total.astype(BF)
    for k in range(3):
        sent(att.at[0], ats.at[k])


def on_device(tokens, w_query, w_key, w_value, gain, w_out):
    vmem = pl.BlockSpec(memory_space=pltpu.VMEM)
    hbm = pl.BlockSpec(memory_space=pl.ANY)
    dma = pltpu.SemaphoreType.DMA
    return pl.pallas_call(
        kernel,
        name="layer",
        out_shape=jax.ShapeDtypeStruct((SPAN, 640), BF),
        in_specs=[hbm, vmem, vmem, vmem, vmem, hbm],
        out_specs=vmem,
        scratch_shapes=[
            pltpu.VMEM((SPAN, 2560), BF),
            pltpu.VMEM((2, Z, X, TILES[0], 16, E), BF),
            pltpu.VMEM((2, Z, X, TILES[1], 16, E), BF),
            pltpu.VMEM((Z, SPAN, E), BF),
            pltpu.VMEM((4, Z, SPAN, E), BF),
            pltpu.VMEM((2, X, 432, 256), BF),
            pltpu.VMEM((COLS, SPAN, E), F32),
            pltpu.VMEM((Y, 640, 640), BF),
            pltpu.VMEM((COLS, SPAN, E), BF),
            pltpu.VMEM((HEADS, SPAN, E), F32),
            pltpu.VMEM((Y, HEADS, SPAN, E), BF),
            pltpu.VMEM((40, 16, E), BF),
            pltpu.VMEM((40, 16, E), BF),
            pltpu.VMEM((20, 16, E), BF),
            pltpu.VMEM((Z, SHARE, 16, E), BF),
            pltpu.VMEM((SHARE, 16, E), F32),
            pltpu.VMEM((X, SHARE, 16, E), F32),
            pltpu.VMEM((Z, SHARE, 16, E), BF),
            pltpu.VMEM((20, 16, E), BF),
            pltpu.VMEM((40, 16, E), BF),
            dma((2,)), dma((2,)),
            dma((2,)), dma((2, Z)),
            dma((2,)), dma((2, Z)),
            dma((2,)), dma((2, Z, 2)),
            dma((2,)), dma((2, Z)),
            dma((3,)), dma((3,)), dma((3,)), dma((3,)), dma(()),
            dma(()), dma(()),
            dma((OWNERS,)), dma((Z,)),
            dma((3,)), dma((3,)),
            dma((Z,)), dma((OWNERS,)),
            dma(()), dma(()),
            dma((3,)), dma((3, HEADS)), dma(()),
        ],
        compiler_params=pltpu.CompilerParams(
            collective_id=1, has_side_effects=True, vmem_limit_bytes=56 << 20
        ),
    )(tokens, w_query, w_key, w_value, gain.reshape(HEADS, E), w_out)


def solution(mesh):
    placed = (
        P("seq", None),
        P("seq", "section"),
        P("seq", "section"),
        P("seq", "section"),
        P("section"),
        P("section", None),
    )
    return jax.shard_map(
        on_device, mesh=mesh, in_specs=placed, out_specs=P("seq", "section"), check_vma=False
    )
```

time: 108 us -> 96.4 us (0.89); the launches traced: 108 us -> 95 us
  Pallas kernels: 106 us -> 93.2 us
    pallas_call x1, Pallas kernels: 106 us -> 93.2 us  [on_device(): pl.pallas_call(kernel, name='layer', out_shape=jax.ShapeDtypeStruct((SPAN...]
where the time goes in v2:
time: 96.4 us; the launch traced here: 95 us
  Pallas kernels  93.2 us (97%)
  local copies, waits for them, and re-layouts  1.73 us (2%)
    pallas_call x1, Pallas kernels, on_device(): pl.pallas_call(kernel, name='layer', out_shape=jax.ShapeDtypeStruct((SPAN...  93.2 us

profile of v2, /device:TPU:1, one launch (start us, length us, event | category | flops | bytes accessed | tf_op | source)
XLA Modules:
  0.0 95.0 jit_solution(13433504328898916100)
XLA Ops:
  0.0 93.2 %layer.1 = bf16[256,640]{1,0:T(8,128)(2,1)} custom-call(bf16[256,2560]{1,0:T(8,128)(2,1)} %tokens_hbm.1, bf16[20,640]{1,0:T(8,128)(2,1)} %wq.1, bf16[20,640]{1,0:T(8,128)(2,1)} %wk.1, bf16[20,640]{1,0:T(8,128)(2,1)} %wv.1, bf16[5,128]{1,0:T(8,128)(2,1)} %bitcast.1, bf16[640,2560]{1,0:T(8,128)(2,1)} %w_out.1), custom_call_target="tpu_custom_call" | custom-call | tf_op jit(solution)/shard_map/layer/pallas_call | solution.py:496
  93.2 1.7 %copy.8 = bf16[256,640]{1,0:T(8,128)(2,1)} copy(bf16[256,640]{1,0:T(8,128)(2,1)} %layer.1) | data formatting | bytes 655360

commit v3 on v2

--- a/solution.py
+++ b/solution.py
@@ -13,7 +13,7 @@
 FIRST = (0, 2 * HEADS)
 WIDE = (2 * HEADS, HEADS)
 TILES = (13, 7)
-CUT = (3, 2)
+CUT = (2, 2)
 SPAN = 256
 OWNERS, SHARE = 10, 2
 MESH = pl.DeviceIdType.MESH
@@ -28,7 +28,7 @@
 def kernel(
     tokens_hbm, wq, wk, wv, gain, w_out, out, tokens,
     G0, G1, T1, T2, PB, acc, wo, kvq, local, att,
-    state, sib_state, chip_sum, zin, xout, xin, pout, pin, pfull,
+    state, sib_state, chip_sum, zin, xout, xin, pout, pfull,
     axs, axr, azs, azr, bzs, bzr, bxs, bxr, ss, sr,
     ws, wr, vs, vr, wl, ps, pr, z1s, z1r, xs, xr, z2s, z2r, qs, qr, ats, atr, tl,
 ):
@@ -140,35 +140,35 @@
         ref = G[ph].at[c, zz(d)]
         return rcopy(ref, ref, ss.at[ph], sr.at[ph, place(d)], sibling)
 
-    def onward(ph, d, copy, ref_of):
-        if d == 0:
-            for delta in (3, -3, 1, -1):
-                copy(ph, 0, delta).start()
-        if abs(d) == 3:
-            for delta in (-d, -d // 3, d // 3):
-                copy(ph, d, delta).start()
-        if abs(d) == 6:
-            for delta in (-d // 6, d // 6):
-                copy(ph, d, delta).start()
+    def onward(ph, d, copy):
+        jumps = {0: (3, -3, 1, -1), 3: (-3, -1, 1), 6: (-1, 1)}.get(abs(d), ())
+        for jump in jumps:
+            copy(ph, d, jump if d >= 0 else -jump).start()
 
     def A(ph, *ds):
         for d in ds:
             ref = ref_a(ph, zz(d))
             rcopy(ref, ref, azs.at[ph], azr.at[ph, place(d)], sibling).wait_recv()
-            onward(ph, d, a_z, ref_a)
+            onward(ph, d, a_z)
         if 6 in ds:
             opposite(ref_a, ph).start()
 
-    def B(ph, *ds):
+    def BZ(ph, *ds):
         for d in ds:
             ref = ref_b(ph, zz(d))
             rcopy(ref, ref, bzs.at[ph], bzr.at[ph, place(d)], sibling).wait_recv()
-            onward(ph, d, b_z, ref_b)
+            onward(ph, d, b_z)
         if 6 in ds:
             opposite(ref_b, ph).start()
+
+    def BX(ph, *ds):
         for d in ds:
             for k in range(3 if late(d) else 2):
                 b_x(ph, d, k).start()
+
+    def B(ph, *ds):
+        BZ(ph, *ds)
+        BX(ph, *ds)
 
     def F(ph, *ds):
         for d in ds:
@@ -182,7 +182,7 @@
 
     def AX(ph):
         a_x_in(ph).wait_recv()
-        onward(ph, 0, a_z, ref_a)
+        onward(ph, 0, a_z)
 
     def w_y(k):
         dev = at(dy=XD[k])
@@ -201,7 +201,7 @@
         )
 
     def begin(ph):
-        onward(ph, 0, b_z, ref_b)
+        onward(ph, 0, b_z)
         for k in range(2):
             b_x(ph, 0, k).start()
 
@@ -285,15 +285,22 @@
     F(0, 2, -2, 4, -4)
     A(0, 2, -2, 4, -4)
     B(0, 5, -5, 7, -7, 8)
+    onward(1, 0, b_z)
+    AX(1)
     S(0, 2, -2, 4, -4)
+    BZ(1, 1, -1)
+    BZ(1, 3, -3)
     M(0, 2, -2, 4, -4)
     S(0, 6, -6)
     A(0, 5, -5, 7, -7, 8)
-    begin(1)
-    AX(1)
+    A(1, 1, -1)
+    A(1, 3, -3)
     M(0, 0, 6, -6)
     S(0, 5, -5)
+    BZ(1, 6, -6)
+    BZ(1, 2, -2, 4, -4)
     S(0, 7, -7, 8)
+    BX(1, 0, 1, -1, 3, -3)
     M(0, 5, -5, 7, -7, 8)
 
     def tile(t):
@@ -309,7 +316,9 @@
         state[pl.ds(8 * h, 8)] = s.astype(BF).reshape(8, 16, E)
     pair1 = rcopy(state, sib_state, ps, pr, sibling)
     pair1.start()
-    B(1, 1, -1, 3, -3)
+    BX(1, 6, -6, 2, -2, 4, -4)
+    A(1, 6, -6)
+    A(1, 2, -2, 4, -4)
     pair1.wait_recv()
     mine = pl.ds(20 * c, 20)
     chip_sum[...] = (state[mine].astype(F32) + sib_state[mine].astype(F32)).astype(BF)
@@ -320,7 +329,7 @@
     def z1(i):
         dst = owner_z(i)
         return rcopy(
-            chip_sum.at[pl.ds(SHARE * i, SHARE)], zin.at[z], z1s.at[i], z1r.at[z],
+            chip_sum.at[pl.ds(SHARE * i, SHARE)], zin.at[z], z1s, z1r.at[z],
             (y, (x * Z + dst) * 2 + c),
         )
 
@@ -335,27 +344,24 @@
         def _():
             zin[z] = chip_sum[pl.ds(SHARE * i, SHARE)]
 
-    F(1, 0)
-    A(1, 1, -1, 3, -3)
-    F(1, 1, -1, 3, -3)
-    B(1, 6, -6, 2, -2, 4, -4)
-    S(1, 0, 1, -1, 3, -3)
-    M(1, 1, -1, 3, -3)
+    BZ(1, 5, -5, 7, -7, 8)
+    BX(1, 5, -5, 7, -7, 8)
+    F(1, 0, 1, -1, 3, -3)
 
     def x_copy(k):
         return rcopy(xout, xin.at[x], xs.at[k], xr.at[k], at(dx=XD[k]))
 
     def z1_in(src):
-        return rcopy(chip_sum.at[pl.ds(0, SHARE)], zin.at[src], z1s.at[0], z1r.at[src], sibling)
+        return rcopy(chip_sum.at[pl.ds(0, SHARE)], zin.at[src], z1s, z1r.at[src], sibling)
 
     def z2(dst):
         return rcopy(
-            pout.at[dst], pin.at[pl.ds(SHARE * my_i, SHARE)], z2s.at[dst], z2r.at[my_i],
+            pout.at[dst], pfull.at[pl.ds(20 * c + SHARE * my_i, SHARE)], z2s, z2r.at[my_i],
             (y, (x * Z + dst) * 2 + c),
         )
 
     def z2_in(i):
-        return rcopy(pout.at[0], pin.at[pl.ds(SHARE * i, SHARE)], z2s.at[0], z2r.at[i], sibling)
+        return rcopy(pout.at[0], pfull.at[pl.ds(20 * c + SHARE * i, SHARE)], z2s, z2r.at[i], sibling)
 
     @pl.when(is_owner)
     def _():
@@ -370,10 +376,9 @@
         for k in range(3):
             x_copy(k).start()
 
+    S(1, 0, 1, -1, 3, -3)
     F(1, 6, -6, 2, -2, 4, -4)
-    A(1, 6, -6, 2, -2, 4, -4)
-    B(1, 5, -5, 7, -7, 8)
-    S(1, 2, -2, 4, -4)
+    M(1, 1, -1, 3, -3)
 
     @pl.when(is_owner)
     def _():
@@ -389,13 +394,14 @@
             @pl.when(dst != z)
             def _():
                 z2(dst).start()
-        pin[pl.ds(SHARE * my_i, SHARE)] = pout[z]
-
-    M(1, 2, -2, 4, -4)
+        pfull[pl.ds(20 * c + SHARE * my_i, SHARE)] = pout[z]
+
+    S(1, 2, -2, 4, -4)
     S(1, 6, -6)
     A(1, 5, -5, 7, -7, 8)
+    S(1, 5, -5, 7, -7, 8)
+    M(1, 2, -2, 4, -4)
     M(1, 0, 6, -6)
-    S(1, 5, -5, 7, -7, 8)
     M(1, 5, -5, 7, -7, 8)
     for k in range(3):
         w_y(k).wait_recv()
@@ -409,35 +415,50 @@
         scores = lax.dot_general(q, k, (((1,), (1,)), ((), ())), preferred_element_type=F32)
         local[h] = dot(jnp.where(causal, scores, 0.0).astype(BF), v)
 
-    for i in range(OWNERS):
-        @pl.when(z != owner_z(i))
-        def _():
-            z2_in(i).wait_recv()
-    pair2 = rcopy(pin, pfull.at[pl.ds(20 * c, 20)], qs, qr, sibling)
-    pair2.start()
-    pfull[mine] = pin[...]
-    pair2.wait_recv()
-
-    def a_y(k, h):
+    def a_y(k, n, h):
         ref = att.at[y, h]
-        return rcopy(ref, ref, ats.at[k], atr.at[c if k == 0 else 1 - c, h], at(dy=XD[k]))
-
-    def a_y_on(h):
-        ref = att.at[lax.rem(y - way + Y, Y), h]
-        return rcopy(ref, ref, ats.at[2], atr.at[2, h], at(dy=way))
-
-    def a_y_in(kind, h):
-        return rcopy(att.at[y, h], att.at[y, h], ats.at[0], atr.at[kind, h], sibling)
-
-    for h in range(HEADS):
+        return rcopy(ref, ref, ats.at[k], atr.at[c if k == 0 else 1 - c, n], at(dy=XD[k]))
+
+    def a_y_on(n):
+        ref = att.at[lax.rem(y - way + Y, Y), nth(n)]
+        return rcopy(ref, ref, ats.at[2], atr.at[2, n], at(dy=way))
+
+    def a_y_in(kind, n):
+        return rcopy(att.at[y, 0], att.at[y, 0], ats.at[0], atr.at[kind, n], sibling)
+
+    def nth(n):
+        return lax.rem(n + 3 * c, HEADS)
+
+    def pair2(n):
+        first, size = (4 * c, 8) if n == 0 else ((4 * c + 8, 8) if n == 1 else (16 * (1 - c), 4))
+        ref = pfull.at[pl.ds(20 * c + first, size)]
+        return rcopy(ref, ref, qs.at[n], qr.at[n], sibling)
+
+    def combine(n):
+        h = nth(n)
         before = pfull[pl.ds(8 * h, 8)].reshape(E, E).astype(F32)
         first = sib_state[pl.ds(8 * h, 8)].reshape(E, E).astype(F32)
         prefix = jnp.where(c == 1, before + first, before).astype(BF)
         combined = dot(kvq[2 * HEADS + h], prefix) + local[h]
         scale = lax.rsqrt(jnp.mean(combined * combined, axis=-1, keepdims=True) + 1e-05)
-        att[y, h] = (combined * scale * gain[h:h + 1].astype(F32)).astype(BF)
+        att[y, h] = (combined * scale * gain[h]).astype(BF)
         for k in range(2):
-            a_y(k, h).start()
+            a_y(k, n, h).start()
+
+    for n, order in enumerate(((0, 1, 2, 3), (4, 5, 6, 7), (8, 9))):
+        for i in order:
+            i = lax.rem(i + 2 * c, OWNERS)
+
+            @pl.when(z != lax.div(i * Z, OWNERS))
+            def _():
+                z2_in(i).wait_recv()
+        pair2(n).start()
+        if n < 2:
+            combine(n)
+    for n in range(3):
+        pair2(n).wait_recv()
+    for n in range(2, HEADS):
+        combine(n)
 
     def project(section):
         lhs = jnp.concatenate([att[section, h] for h in range(HEADS)], axis=1)
@@ -446,9 +467,9 @@
     for k in range(3):
         w_s(k).wait_recv()
     total = tokens[:, pl.ds(pl.multiple_of(640 * y, 128), 640)].astype(F32) + project(y)
-    for h in range(HEADS):
-        a_y_in(0, h).wait_recv()
-        a_y_on(h).start()
+    for n in range(HEADS):
+        a_y_in(0, n).wait_recv()
+        a_y_on(n).start()
     total = total + project(lax.rem(y - way + Y, Y))
 
     for k in range(3):
@@ -465,24 +486,22 @@
         sent(G[ph].at[c, :, pl.ds(0, 3), part_b(ph)], bxs.at[ph])
         sent(G[ph].at[c], ss.at[ph])
     pair1.wait_send()
-    pair2.wait_send()
-    for i in range(OWNERS):
-        @pl.when(z != owner_z(i))
-        def _():
-            z1(i).wait_send()
-
+    for n in range(3):
+        pair2(n).wait_send()
     @pl.when(is_owner)
     def _():
+        sent(chip_sum.at[pl.ds(0, SHARE * (OWNERS - 1))], z1s)
+        sent(pout.at[pl.ds(0, Z - 1)], z2s)
         for k in range(3):
             x_copy(k).wait_send()
-        for dst in range(Z):
-            @pl.when(dst != z)
-            def _():
-                z2(dst).wait_send()
+
+    @pl.when(jnp.logical_not(is_owner))
+    def _():
+        sent(chip_sum, z1s)
 
     for kind, section in ((1, y + way), (2, y + 2)):
-        for h in range(HEADS):
-            a_y_in(kind, h).wait_recv()
+        for n in range(HEADS):
+            a_y_in(kind, n).wait_recv()
         total = total + project(lax.rem(section + Y, Y))
     out[...] = total.astype(BF)
     for k in range(3):
@@ -518,7 +537,6 @@
             pltpu.VMEM((SHARE, 16, E), F32),
             pltpu.VMEM((X, SHARE, 16, E), F32),
             pltpu.VMEM((Z, SHARE, 16, E), BF),
-            pltpu.VMEM((20, 16, E), BF),
             pltpu.VMEM((40, 16, E), BF),
             dma((2,)), dma((2,)),
             dma((2,)), dma((2, Z)),
@@ -527,16 +545,16 @@
             dma((2,)), dma((2, Z)),
             dma((3,)), dma((3,)), dma((3,)), dma((3,)), dma(()),
             dma(()), dma(()),
-            dma((OWNERS,)), dma((Z,)),
+            dma(()), dma((Z,)),
             dma((3,)), dma((3,)),
-            dma((Z,)), dma((OWNERS,)),
-            dma(()), dma(()),
+            dma(()), dma((OWNERS,)),
+            dma((3,)), dma((3,)),
             dma((3,)), dma((3, HEADS)), dma(()),
         ],
         compiler_params=pltpu.CompilerParams(
             collective_id=1, has_side_effects=True, vmem_limit_bytes=56 << 20
         ),
-    )(tokens, w_query, w_key, w_value, gain.reshape(HEADS, E), w_out)
+    )(tokens, w_query, w_key, w_value, gain.astype(F32).reshape(HEADS, 1, E), w_out)
 
 
 def solution(mesh):

time: 96.4 us -> 90.3 us (0.937)
  Pallas kernels: 93.2 us -> 86.6 us
  local copies, waits for them, and re-layouts: 1.73 us -> 3 us
    pallas_call x1, Pallas kernels: 93.2 us -> 86.6 us  [on_device(): pl.pallas_call(kernel, name='layer', out_shape=jax.ShapeDtypeStruct((SPAN...]
    reshape x0 -> x1, local copies, waits for them, and re-layouts: none -> 1.27 us  [on_device(): gain.astype(F32).reshape(HEADS, 1, E)]
where the time goes in v3:
time: 90.3 us; the launch traced here: 89.6 us
  Pallas kernels  86.6 us (96%)
  local copies, waits for them, and re-layouts  3 us (3%)
    pallas_call x1, Pallas kernels, on_device(): pl.pallas_call(kernel, name='layer', out_shape=jax.ShapeDtypeStruct((SPAN...  86.6 us

profile of v3, /device:TPU:1, one launch (start us, length us, event | category | flops | bytes accessed | tf_op | source)
XLA Modules:
  0.0 89.6 jit_solution(8322125534588935492)
XLA Ops:
  0.0 1.3 %reshape.8.gain = f32[5,1,128]{2,1,0:T(1,128)} reshape(bf16[640]{0:T(1024)(128)(2,1)} %param.10) | data formatting | bytes 3840 | tf_op jit(solution)/shard_map/reshape | solution.py:557
  1.3 86.6 %layer.1 = bf16[256,640]{1,0:T(8,128)(2,1)} custom-call(bf16[256,2560]{1,0:T(8,128)(2,1)} %tokens_hbm.1, bf16[20,640]{1,0:T(8,128)(2,1)} %wq.1, bf16[20,640]{1,0:T(8,128)(2,1)} %wk.1, bf16[20,640]{1,0:T(8,128)(2,1)} %wv.1, f32[5,1,128]{2,1,0:T(1,128)} %reshape.8.gain, bf16[640,2560]{1,0:T(8,128)(2,1)} %w_out.1), custom_call_target="tpu_custom_call" | custom-call | tf_op jit(solution)/shard_map/layer/pallas_call | solution.py:515
  87.9 1.7 %copy.8 = bf16[256,640]{1,0:T(8,128)(2,1)} copy(bf16[256,640]{1,0:T(8,128)(2,1)} %layer.1) | data formatting | bytes 655360

commit v4 on v3

--- a/solution.py
+++ b/solution.py
@@ -27,7 +27,7 @@
 
 def kernel(
     tokens_hbm, wq, wk, wv, gain, w_out, out, tokens,
-    G0, G1, T1, T2, PB, acc, wo, kvq, local, att,
+    gain_rows, G0, G1, T1, T2, PB, acc, wo, kvq, local, att,
     state, sib_state, chip_sum, zin, xout, xin, pout, pfull,
     axs, axr, azs, azr, bzs, bzr, bxs, bxr, ss, sr,
     ws, wr, vs, vr, wl, ps, pr, z1s, z1r, xs, xr, z2s, z2r, qs, qr, ats, atr, tl,
@@ -216,6 +216,8 @@
 
     PB[...] = jnp.zeros_like(PB)
     acc[...] = jnp.zeros_like(acc)
+    for h in range(HEADS):
+        gain_rows[h] = gain[h:h + 1].astype(F32)
     row = lax.broadcasted_iota(jnp.int32, (80, 256), 0)
     lane = lax.broadcasted_iota(jnp.int32, (80, 256), 1)
     base = (lane >> 7) * 40 + ((lane >> 6) & 1) * 20
@@ -441,7 +443,7 @@
         prefix = jnp.where(c == 1, before + first, before).astype(BF)
         combined = dot(kvq[2 * HEADS + h], prefix) + local[h]
         scale = lax.rsqrt(jnp.mean(combined * combined, axis=-1, keepdims=True) + 1e-05)
-        att[y, h] = (combined * scale * gain[h]).astype(BF)
+        att[y, h] = (combined * scale * gain_rows[h]).astype(BF)
         for k in range(2):
             a_y(k, n, h).start()
 
@@ -520,6 +522,7 @@
         out_specs=vmem,
         scratch_shapes=[
             pltpu.VMEM((SPAN, 2560), BF),
+            pltpu.VMEM((HEADS, 1, E), F32),
             pltpu.VMEM((2, Z, X, TILES[0], 16, E), BF),
             pltpu.VMEM((2, Z, X, TILES[1], 16, E), BF),
             pltpu.VMEM((Z, SPAN, E), BF),
@@ -554,7 +557,7 @@
         compiler_params=pltpu.CompilerParams(
             collective_id=1, has_side_effects=True, vmem_limit_bytes=56 << 20
         ),
-    )(tokens, w_query, w_key, w_value, gain.astype(F32).reshape(HEADS, 1, E), w_out)
+    )(tokens, w_query, w_key, w_value, gain.reshape(HEADS, E), w_out)
 
 
 def solution(mesh):

time: 90.3 us -> 89.2 us (0.988)
  local copies, waits for them, and re-layouts: 3 us -> 1.73 us
    reshape x1 -> x0, local copies, waits for them, and re-layouts: 1.27 us -> none  [on_device(): gain.astype(F32).reshape(HEADS, 1, E)]
where the time goes in v4:
time: 89.2 us; the launch traced here: 89 us
  Pallas kernels  87.2 us (98%)
  local copies, waits for them, and re-layouts  1.73 us (2%)
    pallas_call x1, Pallas kernels, on_device(): pl.pallas_call(kernel, name='layer', out_shape=jax.ShapeDtypeStruct((SPAN...  87.2 us

profile of v4, /device:TPU:1, one launch (start us, length us, event | category | flops | bytes accessed | tf_op | source)
XLA Modules:
  0.0 89.0 jit_solution(12786432874357431099)
XLA Ops:
  0.0 87.2 %layer.1 = bf16[256,640]{1,0:T(8,128)(2,1)} custom-call(bf16[256,2560]{1,0:T(8,128)(2,1)} %tokens_hbm.1, bf16[20,640]{1,0:T(8,128)(2,1)} %wq.1, bf16[20,640]{1,0:T(8,128)(2,1)} %wk.1, bf16[20,640]{1,0:T(8,128)(2,1)} %wv.1, bf16[5,128]{1,0:T(8,128)(2,1)} %bitcast.1, bf16[640,2560]{1,0:T(8,128)(2,1)} %w_out.1), custom_call_target="tpu_custom_call" | custom-call | tf_op jit(solution)/shard_map/layer/pallas_call | solution.py:517
  87.2 1.7 %copy.8 = bf16[256,640]{1,0:T(8,128)(2,1)} copy(bf16[256,640]{1,0:T(8,128)(2,1)} %layer.1) | data formatting | bytes 655360

commit v5 on v4

--- a/solution.py
+++ b/solution.py
@@ -163,7 +163,7 @@
 
     def BX(ph, *ds):
         for d in ds:
-            for k in range(3 if late(d) else 2):
+            for k in (2, 0, 1) if late(d) else (0, 1):
                 b_x(ph, d, k).start()
 
     def B(ph, *ds):
@@ -392,10 +392,8 @@
         for dst in range(Z):
             pout[dst] = running.astype(BF)
             running = running + zin[dst].astype(F32)
-
-            @pl.when(dst != z)
-            def _():
-                z2(dst).start()
+        for d in (8, 7, 9, 6, 10, 5, 11, 4, 12, 3, 13, 2, 14, 1, 15):
+            z2(zz(d)).start()
         pfull[pl.ds(20 * c + SHARE * my_i, SHARE)] = pout[z]
 
     S(1, 2, -2, 4, -4)

time: 89.2 us -> 89.5 us (level)
  no operation moved by 1% of the time
where the time goes in v5:
time: 89.5 us; the launch traced here: 89.3 us
  Pallas kernels  87.5 us (98%)
  local copies, waits for them, and re-layouts  1.73 us (2%)
    pallas_call x1, Pallas kernels, on_device(): pl.pallas_call(kernel, name='layer', out_shape=jax.ShapeDtypeStruct((SPAN...  87.5 us

profile of v5, /device:TPU:1, one launch (start us, length us, event | category | flops | bytes accessed | tf_op | source)
XLA Modules:
  0.0 89.3 jit_solution(3224426933766891460)
XLA Ops:
  0.0 87.5 %layer.1 = bf16[256,640]{1,0:T(8,128)(2,1)} custom-call(bf16[256,2560]{1,0:T(8,128)(2,1)} %tokens_hbm.1, bf16[20,640]{1,0:T(8,128)(2,1)} %wq.1, bf16[20,640]{1,0:T(8,128)(2,1)} %wk.1, bf16[20,640]{1,0:T(8,128)(2,1)} %wv.1, bf16[5,128]{1,0:T(8,128)(2,1)} %bitcast.1, bf16[640,2560]{1,0:T(8,128)(2,1)} %w_out.1), custom_call_target="tpu_custom_call" | custom-call | tf_op jit(solution)/shard_map/layer/pallas_call | solution.py:515
  87.5 1.7 %copy.8 = bf16[256,640]{1,0:T(8,128)(2,1)} copy(bf16[256,640]{1,0:T(8,128)(2,1)} %layer.1) | data formatting | bytes 655360
